TPU v7x, 32 devices: a whole 2x2x4 slice. The times are simulated.
32 devices in a mesh: leaf: 8 (over z, y), rhs: 4 (over x, core).
Axes of the slice: x: 2, y: 2, z: 4, core: 2. Of those that a mesh axis runs over, the one named last changes fastest.
Arguments:
- points: bfloat16 [64, 65536], P('rhs', 'leaf'), may hold values from -6 to 6
- leaf_basis: bfloat16 [256, 64, 256], P('leaf'), may hold values from -0.375 to 0.375
- local_transfer: bfloat16 [8, 31, 64, 128], P('leaf'), may hold values from -0.625 to 0.625
- top_transfer: bfloat16 [6, 64, 128], replicated, may hold values from -0.625 to 0.625
- leaf_coupling: bfloat16 [3, 256, 64, 320], P(None, 'leaf'), may hold values from -0.3125 to 0.3125
- root_coupling: bfloat16 [3, 8, 64, 192], P(None, 'leaf'), may hold values from -0.4375 to 0.4375
- upper_coupling: bfloat16 [3, 6, 64, 192], replicated, may hold values from -0.4375 to 0.4375
- near_blocks: bfloat16 [3, 256, 3, 256, 256], P(None, 'leaf', None, 'rhs'), may hold values from -0.21875 to 0.21875
- near_offset: int32 [256, 3], P('leaf'), may hold values from -8 to 8, as said below
- far_offset: int32 [256, 5], P('leaf'), may hold values from -8 to 8, as said below
Outputs:
- applied: bfloat16 [3, 64, 65536], P(None, 'rhs', 'leaf')
Inputs may be any that keep to these rules, and one draw needn't show every extreme that they name: `near_offset`: the first entry of each row is 0; the entries of a row are distinct and lie within 8 of 0. `far_offset`: entries are nonzero, distinct within a row, and differ from every entry of the same row of near_offset.
All inputs are finite; a program needn't handle non-finite values.
Results may differ from a plain program's by a relative error of at most 0.025.
Values may be sent and summed in bfloat16 or wider, within the bound.
A program may use at most 192 MiB of HBM per device.

v0:
```python
import jax
import jax.numpy as jnp
from jax import lax
from jax.sharding import PartitionSpec as P

LEAF = 256
OPS = 3
W = 8
NEAR = 3
FAR = 5
TOPL = 3


def from_behind(block, axis, distance):
    devices = range(lax.axis_size(axis))
    route = [(i - distance, i) for i in devices if i - distance in devices]
    return lax.ppermute(block, axis, route)


def swapped(value, axis, distance):
    mask = 2**distance
    pairs = [(source, source ^ mask) for source in range(lax.axis_size(axis))]
    return lax.ppermute(value, axis, pairs)


def with_halo(cells, sides, width):
    for axis, dim in sides:
        count = lax.axis_size(axis)
        ends = count - 1
        head = lax.slice_in_dim(cells, 0, width, axis=dim)
        tail = lax.slice_in_dim(cells, cells.shape[dim] - width, cells.shape[dim], axis=dim)
        cells = jnp.concatenate(
            [
                lax.ppermute(tail, axis, [(i, (i + 1) % count) for i in range(ends)]),
                cells,
                lax.ppermute(head, axis, [((i + 1) % count, i) for i in range(ends)]),
            ],
            axis=dim,
        )
    return cells


def round_half(values):
    return values.astype(jnp.bfloat16)


def pair_up(level_coef, transfer):
    col_count, cluster_count, rank_size = level_coef.shape
    joined = level_coef.reshape(col_count, cluster_count // 2, 2 * rank_size)
    return round_half(
        jnp.einsum("cpk,prk->cpr", joined, transfer, preferred_element_type=jnp.float32)
    )


def pair_down(field, transfer):
    ops_count, col_count, cluster_count, rank_size = field.shape
    children = jnp.einsum(
        "ocpr,prk->ocpk", round_half(field), transfer, preferred_element_type=jnp.float32
    )
    return children.reshape(ops_count, col_count, 2 * cluster_count, rank_size)


def parity_sources(pieces, cluster):
    even_side = jnp.concatenate([pieces[-2], pieces[2], pieces[3]], axis=-1)
    odd_side = jnp.concatenate([pieces[-3], pieces[-2], pieces[2]], axis=-1)
    return jnp.where(cluster % 2 == 0, even_side, odd_side)


def couple_top(sources, coupling):
    return jnp.einsum("ck,ork->ocr", sources, coupling, preferred_element_type=jnp.float32)


def per_device(
    points,
    leaf_basis,
    local_transfer,
    top_transfer,
    leaf_coupling,
    root_coupling,
    upper_coupling,
    near_blocks,
    near_offset,
    far_offset,
):
    col_count, point_count = points.shape
    leaf_count = leaf_basis.shape[0]
    rank_size = leaf_basis.shape[1]
    groups = lax.axis_size("leaf")
    device = lax.axis_index("leaf")

    def top_rows(height):
        return groups - groups // 2 ** (height - 1)

    def coupling_at(height, cluster):
        if height == 0:
            return root_coupling[:, 0]
        return lax.dynamic_index_in_dim(
            upper_coupling, top_rows(height) + cluster, 1, keepdims=False
        )

    leaf_points = points.reshape(col_count, leaf_count, LEAF)
    leaf_coef = round_half(
        jnp.einsum("cti,tri->ctr", leaf_points, leaf_basis, preferred_element_type=jnp.float32)
    )
    depth_local = leaf_count.bit_length() - 1
    transfers = []
    current = leaf_coef
    offset = 0
    for height in range(depth_local):
        cluster_count = leaf_count >> height + 1
        transfer = local_transfer[0, offset : offset + cluster_count]
        transfers.append(transfer)
        current = pair_up(current, transfer)
        offset += cluster_count
    root_coef = current[:, 0]
    fields = []
    ancestor = root_coef
    for height in range(TOPL):
        cluster = device >> height
        pieces = {}
        for cousin in (-3, -2, 2, 3):
            distance = -cousin * 2**height
            if abs(distance) < groups:
                pieces[cousin] = from_behind(ancestor, "leaf", distance)
            else:
                pieces[cousin] = jnp.zeros_like(ancestor)
        fields.append(couple_top(parity_sources(pieces, cluster), coupling_at(height, cluster)))
        if height + 1 < TOPL:
            partner = swapped(ancestor, "leaf", height)
            joined = jnp.where(
                cluster % 2 == 0,
                jnp.concatenate([ancestor, partner], axis=-1),
                jnp.concatenate([partner, ancestor], axis=-1),
            )
            parent_transfer = lax.dynamic_index_in_dim(
                top_transfer, top_rows(height + 1) + (cluster >> 1), 0, keepdims=False
            )
            ancestor = round_half(
                jnp.einsum("ck,rk->cr", joined, parent_transfer, preferred_element_type=jnp.float32)
            )
    running = fields[TOPL - 1]
    for height in range(TOPL - 1, 0, -1):
        cluster = device >> height
        transfer = lax.dynamic_index_in_dim(
            top_transfer, top_rows(height) + cluster, 0, keepdims=False
        )
        pushed = jnp.einsum(
            "ocr,rk->ock", round_half(running), transfer, preferred_element_type=jnp.float32
        )
        child_side = (device >> height - 1) % 2
        pushed_half = lax.dynamic_slice_in_dim(pushed, child_side * rank_size, rank_size, 2)
        running = fields[height - 1] + pushed_half
    field = running[:, :, None, :]
    for height in reversed(range(depth_local)):
        field = pair_down(field, transfers[height])
    leaf_range = jnp.arange(leaf_count, dtype=jnp.int32)[:, None]
    flat_coef = leaf_coef.reshape(col_count, leaf_count * rank_size)
    wide_coef = with_halo(flat_coef, (("leaf", 1),), W * rank_size).reshape(
        col_count, leaf_count + 2 * W, rank_size
    )
    far_index = W + leaf_range + far_offset
    sources = jnp.take(wide_coef, far_index.reshape(-1), axis=1).reshape(
        col_count, leaf_count, FAR * rank_size
    )
    coupled = jnp.einsum(
        "ctk,otrk->octr", sources, leaf_coupling, preferred_element_type=jnp.float32
    )
    leaf_field = round_half(field + coupled)
    far_part = jnp.einsum(
        "octr,tri->octi", leaf_field, leaf_basis, preferred_element_type=jnp.float32
    )
    wide_points = with_halo(points, (("leaf", 1),), W * LEAF).reshape(
        col_count, leaf_count + 2 * W, LEAF
    )
    near_index = W + leaf_range + near_offset
    all_wide = lax.all_gather(wide_points, "rhs", axis=0, tiled=True)
    all_columns = jnp.take(all_wide, near_index.reshape(-1), axis=1).reshape(
        all_wide.shape[0], leaf_count, NEAR, LEAF
    )
    row_terms = jnp.einsum(
        "ctkj,otkij->octi", all_columns, near_blocks, preferred_element_type=jnp.float32
    )
    near_part = lax.all_to_all(row_terms, "rhs", split_axis=1, concat_axis=3, tiled=True)
    result = (far_part + near_part).astype(jnp.bfloat16)
    return result.reshape(OPS, col_count, point_count)


def solution(mesh):
    placed = (
        P("rhs", "leaf"),
        P("leaf", None, None),
        P("leaf", None, None, None),
        P(),
        P(None, "leaf", None, None),
        P(None, "leaf", None, None),
        P(),
        P(None, "leaf", None, "rhs", None),
        P("leaf", None),
        P("leaf", None),
    )
    return jax.shard_map(
        per_device, mesh=mesh, in_specs=placed, out_specs=P(None, "rhs", "leaf"), check_vma=False
    )
```

profile of v0, /device:TPU:0, one launch (start us, length us, event | category | flops | bytes accessed | tf_op | source)
XLA Modules:
  0.0 134.8 jit_solution(9450515656880760610)
XLA Ops:
  6.6 1.0 fusion.162
  7.7 1.3 collective-permute-start.12
  9.0 5.5 %collective-permute-start.11 = (bf16[16,2048]{1,0:T(8,128)(2,1)S(1)}, bf16[16,2048]{1,0:T(8,128)(2,1)S(1)}, u32[]{:S(2)}, u32[]{:S(2)}) collective-permute-start(bf16[16,2048]{1,0:T(8,128)(2,1)S(1)} %get-tuple-element.9), channel_id=1, source_target_pairs={{0,4},{4,8},{8,12},{12,16},{16,20},{20,24},{24,28},{1,5},{5,9},{9,... | collective-permute-start | bytes 196616 | tf_op jit(solution)/shard_map/ppermute | solution.py:34
  14.5 1.3 fusion.24
  15.9 0.1 reshape.144
  16.0 1.2 fusion.26
  17.2 0.1 reshape.145
  17.3 1.1 fusion.28
  18.4 0.1 reshape.146
  18.5 1.0 fusion.34
  19.6 0.1 fusion.39
  19.9 0.8 copy.202
  20.7 0.1 convolution_convert_fusion.11
  20.8 2.9 %collective-permute-start.4 = (bf16[16,64]{1,0:T(8,128)(2,1)S(1)}, bf16[16,64]{1,0:T(8,128)(2,1)S(1)}, u32[]{:S(2)}, u32[]{:S(2)}) collective-permute-start(bf16[16,64]{1,0:T(8,128)(2,1)S(1)} %convolution_convert_fusion.11), channel_id=1, source_target_pairs={{0,4},{4,0},{8,12},{12,8},{16,20},{20,16},{24,28},{28,24},{1,5},{5... | collective-permute-start | bytes 6152 | tf_op jit(solution)/shard_map/ppermute | solution.py:23
  23.7 1.3 collective-permute-start.2
  25.0 0.2 reshape.151
  25.2 0.1 copy.140
  25.3 0.1 reshape.155
  25.5 0.1 reshape.153
  25.7 1.2 fusion.36
  26.9 0.6 fusion.163
  27.5 0.2 convolution_convert_fusion.10
  27.7 1.3 collective-permute-start.7
  29.0 1.3 collective-permute-start.6
  30.3 5.4 %collective-permute-start.5 = (bf16[16,64]{1,0:T(8,128)(2,1)S(1)}, bf16[16,64]{1,0:T(8,128)(2,1)S(1)}, u32[]{:S(2)}, u32[]{:S(2)}) collective-permute-start(bf16[16,64]{1,0:T(8,128)(2,1)S(1)} %convolution_convert_fusion.10), channel_id=1, source_target_pairs={{0,16},{4,20},{8,24},{12,28},{1,17},{5,21},{9,25},{13,29},{2,18},{... | collective-permute-start | bytes 6152 | tf_op jit(solution)/shard_map/ppermute | solution.py:17
  35.7 2.2 %collective-permute-start.8 = (bf16[16,64]{1,0:T(8,128)(2,1)S(1)}, bf16[16,64]{1,0:T(8,128)(2,1)S(1)}, u32[]{:S(2)}, u32[]{:S(2)}) collective-permute-start(bf16[16,64]{1,0:T(8,128)(2,1)S(1)} %convolution_convert_fusion.10), channel_id=1, source_target_pairs={{0,24},{4,28},{1,25},{5,29},{2,26},{6,30},{3,27},{7,31}} | collective-permute-start | bytes 6152 | tf_op jit(solution)/shard_map/ppermute | solution.py:17
  37.9 0.1 copy.138
  38.1 0.1 copy.130
  38.2 0.1 broadcast_in_dim.26
  38.3 0.1 broadcast_in_dim.27
  38.4 1.3 collective-permute-start.1
  39.7 4.5 %collective-permute-start = (bf16[16,64]{1,0:T(8,128)(2,1)S(1)}, bf16[16,64]{1,0:T(8,128)(2,1)S(1)}, u32[]{:S(2)}, u32[]{:S(2)}) collective-permute-start(bf16[16,64]{1,0:T(8,128)(2,1)S(1)} %convolution_convert_fusion.11), channel_id=1, source_target_pairs={{0,8},{4,12},{8,16},{12,20},{16,24},{20,28},{1,9},{5,13},{9,17},{1... | collective-permute-start | bytes 6152 | tf_op jit(solution)/shard_map/ppermute | solution.py:17
  44.3 3.4 %collective-permute-start.3 = (bf16[16,64]{1,0:T(8,128)(2,1)S(1)}, bf16[16,64]{1,0:T(8,128)(2,1)S(1)}, u32[]{:S(2)}, u32[]{:S(2)}) collective-permute-start(bf16[16,64]{1,0:T(8,128)(2,1)S(1)} %convolution_convert_fusion.11), channel_id=1, source_target_pairs={{0,12},{4,16},{8,20},{12,24},{16,28},{1,13},{5,17},{9,21},{13,25},... | collective-permute-start | bytes 6152 | tf_op jit(solution)/shard_map/ppermute | solution.py:17
  47.7 1.3 collective-permute-start.10
  49.0 1.2 fusion.38
  50.2 4.5 %collective-permute-start.9 = (bf16[16,512]{1,0:T(8,128)(2,1)S(1)}, bf16[16,512]{1,0:T(8,128)(2,1)S(1)}, u32[]{:S(2)}, u32[]{:S(2)}) collective-permute-start(bf16[16,512]{1,0:T(8,128)(2,1)S(1)} %get-tuple-element.11), channel_id=1, source_target_pairs={{0,4},{4,8},{8,12},{12,16},{16,20},{20,24},{24,28},{1,5},{5,9},{9,... | collective-permute-start | bytes 49160 | tf_op jit(solution)/shard_map/ppermute | solution.py:34
  54.8 0.3 fusion.37
  55.1 0.1 convert_element_type.120
  55.2 0.1 fusion.29
  55.5 3.9 %gather_fusion.1 = bf16[96,64,256]{2,1,0:T(8,128)(2,1)} fusion(bf16[64,48,256]{2,0,1:T(8,128)(2,1)} %all-gather.2.cloned.1.call-done, s32[1024]{0:T(1024)S(1)} %pad_clamp_fusion), kind=kCustom, calls=%fused_computation.1 | custom fusion | bytes 6291840 | tf_op jit(solution)/shard_map/jit(_take)/gather | solution.py:177
  59.4 8.3 %fusion.7 = f32[3,64,32,64]{3,1,0,2:T(8,128)S(1)} fusion(bf16[3,32,3,64,256]{4,3,2,1,0:T(8,128)(2,1)} %param.17, bf16[64,32,3,256]{3,0,2,1:T(8,128)(2,1)} %bitcast.188, pred[32,3]{1,0:T(8,128)(4,1)S(1)} %copy.138), kind=kOutput, calls=%fused_computation.10 | convolution fusion | flops 605552640 | bytes 14155872 | tf_op jit(solution)/shard_map/ctkj,otkij->octi/dot_general | solution.py:180
  67.7 3.5 %copy.203 = f32[3,64,32,64]{3,2,0,1:T(8,128)} copy(f32[3,64,32,64]{3,1,0,2:T(8,128)S(1)} %fusion.7) | data formatting | bytes 3145728 | tf_op jit(solution)/shard_map/ctkj,otkij->octi/transpose | solution.py:180
  71.2 4.8 %reshape.187 = f32[4,1,98304]{2,1,0:T(1,128)} reshape(f32[64,3,32,64]{3,2,1,0:T(8,128)} %bitcast.185) | data formatting | bytes 3145728
  76.0 3.7 %all-to-all-start = ((f32[4,1,98304]{2,1,0:T(1,128)}), f32[4,1,98304]{2,1,0:T(1,128)S(1)}, u32[]{:S(2)}, u32[]{:S(2)}) async-start(f32[4,1,98304]{2,1,0:T(1,128)} %reshape.187), calls=%async_computation | async-start | bytes 3145728 | tf_op jit(solution)/shard_map/all_to_all | solution.py:183
  79.8 0.2 fusion.27
  79.9 0.1 convert_element_type.126
  80.0 0.2 fusion.25
  80.3 0.1 convert_element_type.129
  80.4 0.2 convolution_bitcast_fusion
  80.6 0.1 copy.129
  80.8 1.1 reshape.150
  81.9 0.2 reshape.152
  82.1 0.7 gather_fusion
  82.8 1.0 copy.134
  83.9 1.6 %gather.13 = bf16[16,32,320]{2,1,0:T(8,128)(2,1)S(1)} reshape(bf16[16,160,64]{2,1,0:T(8,128)(2,1)} %copy.134) | data formatting | bytes 655360 | tf_op jit(solution)/shard_map/jit(_take)/gather | solution.py:162
  85.4 0.8 select_bitcast_fusion
  86.2 13.4 %all-to-all-done = f32[4,1,98304]{2,1,0:T(1,128)S(1)} async-done(((f32[4,1,98304]{2,1,0:T(1,128)}), f32[4,1,98304]{2,1,0:T(1,128)S(1)}, u32[]{:S(2)}, u32[]{:S(2)}) %all-to-all-start) | async-done | bytes 1572896 | tf_op jit(solution)/shard_map/all_to_all | solution.py:183
  99.6 0.5 broadcast.92
  100.2 6.4 %reduce = f32[4,98304]{1,0:T(4,128)} reduce(f32[4,1,98304]{2,1,0:T(1,128)S(1)} %all-to-all-done, f32[]{:T(128)} %broadcast.92), dimensions={1}, to_apply=%all_to_all.13.reduce_sub_computation | reduce | bytes 3145732 | tf_op jit(solution)/shard_map/all_to_all | solution.py:183
  106.5 4.5 %reshape.188 = f32[64,3,32,64]{3,2,1,0:T(8,128)} reshape(f32[4,98304]{1,0:T(4,128)} %reduce) | data formatting | bytes 3145728
  111.0 5.6 %copy.201 = f32[3,4,16,32,64]{4,1,2,0,3:T(4,128)} copy(f32[3,4,16,32,64]{4,3,0,2,1:T(8,128)} %bitcast.186) | data formatting | bytes 3145728 | tf_op jit(solution)/shard_map/all_to_all | solution.py:183
  116.6 3.3 %all_to_all.16 = f32[3,16,32,256]{3,1,0,2:T(8,128)S(1)} reshape(f32[3,16,32,4,64]{4,3,1,0,2:T(4,128)} %bitcast.187) | data formatting | bytes 3145728 | tf_op jit(solution)/shard_map/all_to_all | solution.py:183
  120.0 5.9 %fusion.14 = bf16[32,3,2,8,256]{4,3,2,1,0:T(8,128)(2,1)} fusion(f32[3,16,32,256]{3,1,0,2:T(8,128)S(1)} %all_to_all.16, bf16[32,64,256]{2,1,0:T(8,128)(2,1)S(1)} %copy-done, bf16[3,32,64,320]{3,2,1,0:T(8,128)(2,1)} %param.14, f32[3,16,32,64]{3,2,1,0:T(8,128)S(1)} %copy-done.1, bf16[16,32,320,1]{2,1,0,3:T(8,128)(2,1)} %select_bitcast_fusion), kind=kOutput, calls=%fused_computation.14 | convolution fusion | flops 114229248 | bytes 8060928 | tf_op jit(solution)/shard_map/octr,tri->octi/dot_general | solution.py:169
  125.9 2.1 %copy.157 = bf16[32,3,2,8,256]{4,3,0,2,1:T(8,128)(2,1)} copy(bf16[32,3,2,8,256]{4,3,2,1,0:T(8,128)(2,1)} %fusion.14) | data formatting | bytes 1572864 | tf_op jit(solution)/shard_map/reshape | solution.py:185
  (54 shorter events, 0.9 us)
Async XLA Ops:
  6.5 7.9 %copy-start = (bf16[32,64,256]{2,1,0:T(8,128)(2,1)S(1)}, bf16[32,64,256]{2,1,0:T(8,128)(2,1)}, u32[]{:S(2)}) copy-start(bf16[32,64,256]{2,1,0:T(8,128)(2,1)} %param.11) | copy-start | bytes 3145732
  6.5 13.3 %copy-start.3 = (bf16[16,8192]{1,0:T(8,128)(2,1)S(1)}, bf16[16,8192]{1,0:T(8,128)(2,1)}, u32[]{:S(2)}) copy-start(bf16[16,8192]{1,0:T(8,128)(2,1)} %param.10) | copy-start | bytes 786436
  6.5 13.1 %copy-start.2 = (bf16[1,31,64,128]{3,2,1,0:T(8,128)(2,1)S(1)}, bf16[1,31,64,128]{3,2,1,0:T(8,128)(2,1)}, u32[]{:S(2)}) copy-start(bf16[1,31,64,128]{3,2,1,0:T(8,128)(2,1)} %param.12) | copy-start | bytes 1523716
  6.5 18.7 %copy-start.7 = (s32[32,3]{0,1:T(4,128)S(1)}, s32[32,3]{0,1:T(4,128)}, u32[]{:S(2)}) copy-start(s32[32,3]{0,1:T(4,128)} %param.18) | copy-start | bytes 1156
  6.5 18.9 %copy-start.6 = (s32[32,5]{0,1:T(8,128)S(1)}, s32[32,5]{0,1:T(8,128)}, u32[]{:S(2)}) copy-start(s32[32,5]{0,1:T(8,128)} %param.19) | copy-start | bytes 1924
  6.5 19.1 %copy-start.5 = (bf16[6,64,128]{2,1,0:T(8,128)(2,1)S(1)}, bf16[6,64,128]{2,1,0:T(8,128)(2,1)}, u32[]{:S(2)}) copy-start(bf16[6,64,128]{2,1,0:T(8,128)(2,1)} %param.13) | copy-start | bytes 294916
  6.6 48.2 %copy-start.4 = (bf16[3,1,64,192]{3,2,1,0:T(8,128)(2,1)S(1)}, bf16[3,1,64,192]{3,2,1,0:T(8,128)(2,1)}, u32[]{:S(2)}) copy-start(bf16[3,1,64,192]{3,2,1,0:T(8,128)(2,1)} %param.15) | copy-start | bytes 221188
  6.6 48.9 %all-gather.2.cloned.1.call-start = ((), (), s32[]{:S(2)}) async-start(), calls=%async_computation.1 | async-start | bytes 1966080 | tf_op jit(solution)/shard_map/all_gather | solution.py:176
  7.7 12.2 %collective-permute-start.12 = (bf16[16,2048]{1,0:T(8,128)(2,1)S(1)}, bf16[16,2048]{1,0:T(8,128)(2,1)S(1)}, u32[]{:S(2)}, u32[]{:S(2)}) collective-permute-start(bf16[16,2048]{1,0:T(8,128)(2,1)S(1)} %get-tuple-element.10), channel_id=1, source_target_pairs={{4,0},{8,4},{12,8},{16,12},{20,16},{24,20},{28,24},{5,1},{9,5},{13... | collective-permute-start | bytes 196616 | tf_op jit(solution)/shard_map/ppermute | solution.py:36
  9.0 10.9 %collective-permute-start.11 = (bf16[16,2048]{1,0:T(8,128)(2,1)S(1)}, bf16[16,2048]{1,0:T(8,128)(2,1)S(1)}, u32[]{:S(2)}, u32[]{:S(2)}) collective-permute-start(bf16[16,2048]{1,0:T(8,128)(2,1)S(1)} %get-tuple-element.9), channel_id=1, source_target_pairs={{0,4},{4,8},{8,12},{12,16},{16,20},{20,24},{24,28},{1,5},{5,9},{9,... | collective-permute-start | bytes 196616 | tf_op jit(solution)/shard_map/ppermute | solution.py:34
  20.8 6.7 %collective-permute-start.4 = (bf16[16,64]{1,0:T(8,128)(2,1)S(1)}, bf16[16,64]{1,0:T(8,128)(2,1)S(1)}, u32[]{:S(2)}, u32[]{:S(2)}) collective-permute-start(bf16[16,64]{1,0:T(8,128)(2,1)S(1)} %convolution_convert_fusion.11), channel_id=1, source_target_pairs={{0,4},{4,0},{8,12},{12,8},{16,20},{20,16},{24,28},{28,24},{1,5},{5... | collective-permute-start | bytes 6152 | tf_op jit(solution)/shard_map/ppermute | solution.py:23
  23.7 26.5 %collective-permute-start.2 = (bf16[16,64]{1,0:T(8,128)(2,1)S(1)}, bf16[16,64]{1,0:T(8,128)(2,1)S(1)}, u32[]{:S(2)}, u32[]{:S(2)}) collective-permute-start(bf16[16,64]{1,0:T(8,128)(2,1)S(1)} %convolution_convert_fusion.11), channel_id=1, source_target_pairs={{12,0},{16,4},{20,8},{24,12},{28,16},{13,1},{17,5},{21,9},{25,13},... | collective-permute-start | bytes 6152 | tf_op jit(solution)/shard_map/ppermute | solution.py:17
  27.7 10.7 %collective-permute-start.7 = (bf16[16,64]{1,0:T(8,128)(2,1)S(1)}, bf16[16,64]{1,0:T(8,128)(2,1)S(1)}, u32[]{:S(2)}, u32[]{:S(2)}) collective-permute-start(bf16[16,64]{1,0:T(8,128)(2,1)S(1)} %convolution_convert_fusion.10), channel_id=1, source_target_pairs={{24,0},{28,4},{25,1},{29,5},{26,2},{30,6},{27,3},{31,7}} | collective-permute-start | bytes 6152 | tf_op jit(solution)/shard_map/ppermute | solution.py:17
  29.0 10.7 %collective-permute-start.6 = (bf16[16,64]{1,0:T(8,128)(2,1)S(1)}, bf16[16,64]{1,0:T(8,128)(2,1)S(1)}, u32[]{:S(2)}, u32[]{:S(2)}) collective-permute-start(bf16[16,64]{1,0:T(8,128)(2,1)S(1)} %convolution_convert_fusion.10), channel_id=1, source_target_pairs={{16,0},{20,4},{24,8},{28,12},{17,1},{21,5},{25,9},{29,13},{18,2},{... | collective-permute-start | bytes 6152 | tf_op jit(solution)/shard_map/ppermute | solution.py:17
  30.3 14.0 %collective-permute-start.5 = (bf16[16,64]{1,0:T(8,128)(2,1)S(1)}, bf16[16,64]{1,0:T(8,128)(2,1)S(1)}, u32[]{:S(2)}, u32[]{:S(2)}) collective-permute-start(bf16[16,64]{1,0:T(8,128)(2,1)S(1)} %convolution_convert_fusion.10), channel_id=1, source_target_pairs={{0,16},{4,20},{8,24},{12,28},{1,17},{5,21},{9,25},{13,29},{2,18},{... | collective-permute-start | bytes 6152 | tf_op jit(solution)/shard_map/ppermute | solution.py:17
  35.7 11.9 %collective-permute-start.8 = (bf16[16,64]{1,0:T(8,128)(2,1)S(1)}, bf16[16,64]{1,0:T(8,128)(2,1)S(1)}, u32[]{:S(2)}, u32[]{:S(2)}) collective-permute-start(bf16[16,64]{1,0:T(8,128)(2,1)S(1)} %convolution_convert_fusion.10), channel_id=1, source_target_pairs={{0,24},{4,28},{1,25},{5,29},{2,26},{6,30},{3,27},{7,31}} | collective-permute-start | bytes 6152 | tf_op jit(solution)/shard_map/ppermute | solution.py:17
  38.4 16.3 %collective-permute-start.1 = (bf16[16,64]{1,0:T(8,128)(2,1)S(1)}, bf16[16,64]{1,0:T(8,128)(2,1)S(1)}, u32[]{:S(2)}, u32[]{:S(2)}) collective-permute-start(bf16[16,64]{1,0:T(8,128)(2,1)S(1)} %convolution_convert_fusion.11), channel_id=1, source_target_pairs={{8,0},{12,4},{16,8},{20,12},{24,16},{28,20},{9,1},{13,5},{17,9},{2... | collective-permute-start | bytes 6152 | tf_op jit(solution)/shard_map/ppermute | solution.py:17
  39.7 15.0 %collective-permute-start = (bf16[16,64]{1,0:T(8,128)(2,1)S(1)}, bf16[16,64]{1,0:T(8,128)(2,1)S(1)}, u32[]{:S(2)}, u32[]{:S(2)}) collective-permute-start(bf16[16,64]{1,0:T(8,128)(2,1)S(1)} %convolution_convert_fusion.11), channel_id=1, source_target_pairs={{0,8},{4,12},{8,16},{12,20},{16,24},{20,28},{1,9},{5,13},{9,17},{1... | collective-permute-start | bytes 6152 | tf_op jit(solution)/shard_map/ppermute | solution.py:17
  44.3 10.5 %collective-permute-start.3 = (bf16[16,64]{1,0:T(8,128)(2,1)S(1)}, bf16[16,64]{1,0:T(8,128)(2,1)S(1)}, u32[]{:S(2)}, u32[]{:S(2)}) collective-permute-start(bf16[16,64]{1,0:T(8,128)(2,1)S(1)} %convolution_convert_fusion.11), channel_id=1, source_target_pairs={{0,12},{4,16},{8,20},{12,24},{16,28},{1,13},{5,17},{9,21},{13,25},... | collective-permute-start | bytes 6152 | tf_op jit(solution)/shard_map/ppermute | solution.py:17
  47.7 34.2 %collective-permute-start.10 = (bf16[16,512]{1,0:T(8,128)(2,1)}, bf16[16,512]{1,0:T(8,128)(2,1)S(1)}, u32[]{:S(2)}, u32[]{:S(2)}) collective-permute-start(bf16[16,512]{1,0:T(8,128)(2,1)} %get-tuple-element.12), channel_id=1, source_target_pairs={{4,0},{8,4},{12,8},{16,12},{20,16},{24,20},{28,24},{5,1},{9,5},{13... | collective-permute-start | bytes 49160 | tf_op jit(solution)/shard_map/ppermute | solution.py:36
  50.2 31.7 %collective-permute-start.9 = (bf16[16,512]{1,0:T(8,128)(2,1)S(1)}, bf16[16,512]{1,0:T(8,128)(2,1)S(1)}, u32[]{:S(2)}, u32[]{:S(2)}) collective-permute-start(bf16[16,512]{1,0:T(8,128)(2,1)S(1)} %get-tuple-element.11), channel_id=1, source_target_pairs={{0,4},{4,8},{8,12},{12,16},{16,20},{20,24},{24,28},{1,5},{5,9},{9,... | collective-permute-start | bytes 49160 | tf_op jit(solution)/shard_map/ppermute | solution.py:34
  76.0 23.6 %all-to-all-start = ((f32[4,1,98304]{2,1,0:T(1,128)}), f32[4,1,98304]{2,1,0:T(1,128)S(1)}, u32[]{:S(2)}, u32[]{:S(2)}) async-start(f32[4,1,98304]{2,1,0:T(1,128)} %reshape.187), calls=%async_computation | async-start | bytes 3145728 | tf_op jit(solution)/shard_map/all_to_all | solution.py:183
  116.6 3.3 %copy-start.1 = (f32[3,16,32,64]{3,2,1,0:T(8,128)S(1)}, f32[3,16,32,64]{3,2,1,0:T(8,128)}, u32[]{:S(2)}) copy-start(f32[3,16,32,64]{3,2,1,0:T(8,128)} %reshape.150) | copy-start | bytes 1179652
Sparse Core Ops, SparseCore 0:
  20.8 21.2 all-gather.1
where the time goes:
time: 136 us; the launch traced here: 135 us
  starting transfers between devices  40 us (29%)
  local copies, waits for them, and re-layouts  37.5 us (28%)
  matrix products  22.5 us (17%)
  between operations  13.9 us (10%)
  waiting for transfers between devices  13.4 us (10%)
  other arithmetic  7.29 us (5%)
    ppermute x8, starting transfers between devices, from_behind(): return lax.ppermute(block, axis, route)  20.7 us
    all_to_all x1, waiting for transfers between devices, per_device(): lax.all_to_all(row_terms, 'rhs', split_axis=1, concat_axis=3, tiled=True)  13.4 us
    ppermute x2, starting transfers between devices, with_halo(): lax.ppermute(tail, axis, [(i, (i + 1) % count) for i in range(ends)])  10 us
    all_to_all x3, local copies, waits for them, and re-layouts, per_device(): lax.all_to_all(row_terms, 'rhs', split_axis=1, concat_axis=3, tiled=True)  9.45 us
    unnamed x18, local copies, waits for them, and re-layouts  9.35 us
    dot_general x1, matrix products, per_device(): jnp.einsum('ctkj,otkij->octi', all_columns, near_blocks, preferred_elemen...  8.31 us
    all_to_all x1, other arithmetic, per_device(): lax.all_to_all(row_terms, 'rhs', split_axis=1, concat_axis=3, tiled=True)  6.37 us
    dot_general x1, matrix products, per_device(): jnp.einsum('octr,tri->octi', leaf_field, leaf_basis, preferred_element_ty...  5.87 us
  transfers between devices with their start and end apart: 15, of which 1 were waited for; matrix products, arithmetic and copies ran while one was open for 28% of the time, Pallas kernels for 0%

commit v1 on v0

v1 whole, which is shorter than its diff:
```python
import functools

import jax
import jax.numpy as jnp
from jax import lax
from jax.experimental import pallas as pl
from jax.experimental.pallas import tpu as pltpu
from jax.sharding import PartitionSpec as P

LEAF = 256
OPS = 3
W = 8
NEAR = 3
FAR = 5
TOPL = 3
RHS = 4
CHUNKS = 4
UNROLL = 4
MESH = pl.DeviceIdType.MESH
F32 = jnp.float32
BF16 = jnp.bfloat16


def dot_nt(a, b):
    return lax.dot_general(a, b, (((1,), (1,)), ((), ())), preferred_element_type=F32)


def dot_nn(a, b):
    return lax.dot_general(a, b, (((1,), (0,)), ((), ())), preferred_element_type=F32)


def twice(values):
    return jnp.concatenate([values, values], axis=-1).astype(BF16)


def kernel(
    groups,
    points,
    near_offset,
    far_offset,
    basis_hbm,
    local_hbm,
    top_hbm,
    coupling_hbm,
    root_hbm,
    upper_hbm,
    blocks_hbm,
    out,
    basis,
    local,
    top,
    coupling,
    root_k,
    upper_k,
    blocks,
    wide,
    coef,
    level_coef,
    roots,
    upper_coef,
    coupled,
    fields,
    near_send,
    near_recv,
    in_sem,
    send_sem,
    recv_sem,
    root_send,
    root_recv,
    near_ssem,
    near_rsem,
):
    cols = points.shape[0]
    leaves = basis.shape[0]
    rank = basis.shape[1]
    pairs = leaves // 2
    me_l = lax.axis_index("leaf")
    me_r = lax.axis_index("rhs")
    side = me_r + 1 - 2 * (me_r % 2)
    across = (me_r + 2) % 4
    diagonal = (side + 2) % 4
    peers = (me_r, side, across, diagonal)
    has_left = me_l > 0
    has_right = me_l < groups - 1
    top_w = W + leaves

    loads = [
        pltpu.make_async_copy(source, target, in_sem.at[i])
        for i, (source, target) in enumerate(
            [
                (basis_hbm, basis),
                (local_hbm, local),
                (coupling_hbm, coupling),
                (blocks_hbm, blocks),
                (top_hbm, top),
                (root_hbm, root_k),
                (upper_hbm, upper_k),
            ]
        )
    ]
    for load in loads:
        load.start()

    barrier = pltpu.get_barrier_semaphore()
    for peer in peers[1:]:
        pl.semaphore_signal(barrier, inc=1, device_id=(me_l, peer), device_id_type=MESH)
    for step in range(1, groups):
        pl.semaphore_signal(
            barrier, inc=1, device_id=((me_l + step) % groups, me_r), device_id_type=MESH
        )

    for t in range(leaves):
        wide[0, W + t] = points[:, t * LEAF : (t + 1) * LEAF]
    low, high = pl.ds(0, W), pl.ds(top_w, W)
    head, tail = pl.ds(W, W), pl.ds(leaves, W)
    middle = pl.ds(2 * W, leaves - 2 * W)
    body = pl.ds(W, leaves)

    @pl.when(jnp.logical_not(has_left))
    def _():
        wide[:, 0:W] = jnp.zeros((RHS, W, cols, LEAF), BF16)
        coef[0:W] = jnp.zeros((W, cols, 2 * rank), BF16)

    @pl.when(jnp.logical_not(has_right))
    def _():
        wide[:, top_w : top_w + W] = jnp.zeros((RHS, W, cols, LEAF), BF16)
        coef[top_w : top_w + W] = jnp.zeros((W, cols, 2 * rank), BF16)

    roots[0:3] = jnp.zeros((3, cols, 2 * rank), BF16)
    roots[3 + groups : 6 + groups] = jnp.zeros((3, cols, 2 * rank), BF16)
    upper_coef[...] = jnp.zeros(upper_coef.shape, BF16)

    right = (me_l + 1) % groups
    left = (me_l + groups - 1) % groups

    def remote(number, source, target, leaf, rhs):
        return pltpu.make_async_remote_copy(
            src_ref=source,
            dst_ref=target,
            send_sem=send_sem.at[number],
            recv_sem=recv_sem.at[number],
            device_id=(leaf, rhs),
            device_id_type=MESH,
        )

    def part(slot, where):
        return wide.at[slot, where]

    copies = {
        0: (part(0, head), part(2, head), me_l, across),
        1: (part(0, tail), part(2, tail), me_l, across),
        2: (part(0, middle), part(2, middle), me_l, across),
        3: (part(0, body), part(1, body), me_l, side),
        4: (part(0, tail), part(0, low), right, me_r),
        5: (part(0, head), part(0, high), left, me_r),
        6: (part(2, tail), part(2, low), right, me_r),
        7: (part(2, head), part(2, high), left, me_r),
        8: (part(2, head), part(3, head), me_l, side),
        9: (part(2, tail), part(3, tail), me_l, side),
        10: (part(2, middle), part(3, middle), me_l, side),
        11: (part(0, low), part(1, low), me_l, side),
        12: (part(0, high), part(1, high), me_l, side),
        13: (part(2, low), part(3, low), me_l, side),
        14: (part(2, high), part(3, high), me_l, side),
        15: (coef.at[tail], coef.at[low], right, me_r),
        16: (coef.at[head], coef.at[high], left, me_r),
    }
    to_right = (4, 6, 15)
    to_left = (5, 7, 16)
    from_low = (11, 13)
    from_high = (12, 14)

    def guard(number, receiving):
        if number in to_right:
            return has_left if receiving else has_right
        if number in to_left:
            return has_right if receiving else has_left
        if number in from_low:
            return has_left
        if number in from_high:
            return has_right
        return None

    def run(number, action):
        condition = guard(number, action == "wait_recv")

        def go():
            getattr(remote(number, *copies[number]), action)()

        if condition is None:
            go()
        else:
            pl.when(condition)(go)

    def start(number):
        run(number, "start")

    def arrived(number):
        run(number, "wait_recv")

    pl.semaphore_wait(barrier, len(peers) - 1 + groups - 1)
    for number in (0, 1, 4, 5, 2, 3):
        start(number)

    first_half = lax.broadcasted_iota(jnp.int32, (cols, 2 * rank), 1) < rank

    def joined(a, b):
        return jnp.where(first_half, a.astype(F32), b.astype(F32)).astype(BF16)

    loads[0].wait()

    @pl.loop(0, leaves // UNROLL)
    def _(step):
        for u in range(UNROLL):
            t = step * UNROLL + u
            coef[W + t] = twice(dot_nt(wide[0, W + t], basis[t]))

    start(15)
    start(16)

    arrived(0)
    start(7)
    start(8)
    arrived(1)
    start(6)
    start(9)

    loads[1].wait()
    depth = leaves.bit_length() - 1
    offset = 0
    base = 0
    for height in range(depth):
        count = leaves >> height + 1
        for p in range(count):
            if height == 0:
                pair = joined(coef[W + 2 * p], coef[W + 2 * p + 1])
            else:
                pair = joined(level_coef[base + 2 * p], level_coef[base + 2 * p + 1])
            level_coef[offset + p] = twice(dot_nt(pair, local[0, offset + p]))
        base = offset
        offset += count
    roots[3 + me_l] = level_coef[leaves - 2]

    def root_copy(step):
        return pltpu.make_async_remote_copy(
            src_ref=roots.at[3 + me_l],
            dst_ref=roots.at[3 + me_l],
            send_sem=root_send.at[step - 1],
            recv_sem=root_recv.at[step - 1],
            device_id=((me_l + step) % groups, me_r),
            device_id_type=MESH,
        )

    for step in range(1, groups):
        root_copy(step).start()

    arrived(4)
    start(11)
    arrived(5)
    start(12)
    arrived(15)
    arrived(16)

    loads[2].wait()

    @pl.loop(0, leaves // UNROLL)
    def _(step):
        for u in range(UNROLL):
            t = step * UNROLL + u
            picked = [coef[W + t + far_offset[t, k]] for k in range(FAR)]
            pieces = [joined(picked[k], picked[k + 1]) for k in range(0, FAR - 1, 2)]
            pieces.append(picked[FAR - 1][:, :rank])
            sources = jnp.concatenate(pieces, axis=-1)
            for o in range(OPS):
                coupled[t, o * cols : (o + 1) * cols] = dot_nt(sources, coupling[o, t])

    arrived(6)
    start(13)
    arrived(7)
    start(14)
    arrived(2)
    start(10)
    for number in (3, 8, 9, 11, 12, 13, 14, 10):
        arrived(number)

    loads[3].wait()
    chunk_pairs = pairs // CHUNKS

    def near_copy(chunk, j):
        rows = pl.ds(chunk * chunk_pairs, chunk_pairs)
        return pltpu.make_async_remote_copy(
            src_ref=near_send.at[j, rows],
            dst_ref=near_recv.at[j, rows],
            send_sem=near_ssem.at[chunk, j],
            recv_sem=near_rsem.at[chunk, j],
            device_id=(me_l, peers[j]),
            device_id_type=MESH,
        )

    def near_leaf(t):
        total = None
        for k in range(NEAR):
            left_side = wide[:, W + t + near_offset[t, k]].reshape(RHS * cols, LEAF)
            term = dot_nt(left_side, blocks[:, t, k].reshape(OPS * rank, LEAF))
            total = term if total is None else total + term
        return total

    for chunk in range(CHUNKS):

        @pl.loop(0, chunk_pairs)
        def _(step):
            pair = chunk * chunk_pairs + step
            first = near_leaf(2 * pair)
            second = near_leaf(2 * pair + 1)
            packed = jnp.concatenate(
                [
                    first[:, : 2 * rank],
                    second[:, : 2 * rank],
                    first[:, 2 * rank :],
                    second[:, 2 * rank :],
                ],
                axis=-1,
            ).astype(BF16)
            near_recv[0, pair] = packed[:cols]
            for j in range(1, RHS):
                near_send[j, pair] = packed[j * cols : (j + 1) * cols]

        for j in (2, 3, 1):
            near_copy(chunk, j).start()

    for step in range(1, groups):
        root_copy(step).wait_recv()
    for i in (4, 5, 6):
        loads[i].wait()

    def top_row(height):
        return groups - groups // 2 ** (height - 1)

    def top_base(height):
        return sum(groups // 2**h + 6 for h in range(1, height))

    def top_coef(height, index):
        if height == 0:
            return roots[3 + index]
        return upper_coef[top_base(height) + 3 + index]

    for height in range(1, TOPL):
        for q in range(groups // 2**height):
            pair = joined(top_coef(height - 1, 2 * q), top_coef(height - 1, 2 * q + 1))
            upper_coef[top_base(height) + 3 + q] = twice(dot_nt(pair, top[top_row(height) + q]))

    def top_field(height):
        cluster = me_l // 2**height
        odd = cluster % 2
        near_by = [
            top_coef(height, cluster + s) for s in (-2 - odd, 2 - 4 * odd, 3 - odd)
        ]
        sources = jnp.concatenate([joined(near_by[0], near_by[1]), near_by[2][:, :rank]], axis=-1)
        terms = []
        for o in range(OPS):
            matrix = root_k[o, 0] if height == 0 else upper_k[o, top_row(height) + cluster]
            terms.append(dot_nt(sources, matrix))
        return jnp.concatenate(terms, axis=0)

    running = top_field(TOPL - 1)
    for height in range(TOPL - 1, 0, -1):
        pushed = dot_nn(running.astype(BF16), top[top_row(height) + me_l // 2**height])
        child = (me_l // 2 ** (height - 1)) % 2
        half = jnp.where(child == 0, pushed[:, :rank], pushed[:, rank:])
        running = top_field(height - 1) + half

    fields[1] = running
    for height in reversed(range(depth)):
        count = leaves >> height + 1
        offset = leaves - 2 * count
        for p in range(count):
            pushed = dot_nn(fields[count + p].astype(BF16), local[0, offset + p])
            fields[2 * (count + p)] = pushed[:, :rank]
            fields[2 * (count + p) + 1] = pushed[:, rank:]

    for j in range(1, RHS):
        near_copy(0, j).wait_recv()
    slots = (me_r, side, across, diagonal)
    for chunk in range(CHUNKS):
        if chunk:
            for j in range(1, RHS):
                near_copy(chunk, j).wait_recv()

        for step in range(chunk_pairs):
            pair = chunk * chunk_pairs + step
            near = [near_recv[slots[r], pair].astype(F32) for r in range(RHS)]
            for e in range(2):
                t = 2 * pair + e
                leaf_field = (fields[leaves + t] + coupled[t]).astype(BF16)
                far = dot_nn(leaf_field, basis[t])
                for o in range(OPS):
                    at = (2 * e + o if o < 2 else 4 + e) * rank
                    row = jnp.concatenate([piece[:, at : at + rank] for piece in near], axis=-1)
                    out[o, :, t * LEAF : (t + 1) * LEAF] = (
                        far[o * cols : (o + 1) * cols] + row
                    ).astype(BF16)

    for number in copies:
        run(number, "wait_send")
    for step in range(1, groups):
        root_copy(step).wait_send()
    for chunk in range(CHUNKS):
        for j in range(1, RHS):
            near_copy(chunk, j).wait_send()


def per_device(
    points,
    leaf_basis,
    local_transfer,
    top_transfer,
    leaf_coupling,
    root_coupling,
    upper_coupling,
    near_blocks,
    near_offset,
    far_offset,
):
    groups = lax.axis_size("leaf")
    cols, count = points.shape
    leaves, rank, _ = leaf_basis.shape
    upper_rows = sum(groups // 2**h + 6 for h in range(1, TOPL))
    anywhere = pl.BlockSpec(memory_space=pl.ANY)
    near_shape = (RHS, leaves // 2, cols, 2 * OPS * rank)
    return pl.pallas_call(
        functools.partial(kernel, groups),
        out_shape=jax.ShapeDtypeStruct((OPS, cols, count), BF16),
        in_specs=[
            pl.BlockSpec(memory_space=pltpu.VMEM),
            pl.BlockSpec(memory_space=pltpu.SMEM),
            pl.BlockSpec(memory_space=pltpu.SMEM),
        ]
        + [anywhere] * 7,
        out_specs=pl.BlockSpec(memory_space=pltpu.VMEM),
        scratch_shapes=[
            pltpu.VMEM(leaf_basis.shape, BF16),
            pltpu.VMEM(local_transfer.shape, BF16),
            pltpu.VMEM(top_transfer.shape, BF16),
            pltpu.VMEM(leaf_coupling.shape, BF16),
            pltpu.VMEM(root_coupling.shape, BF16),
            pltpu.VMEM(upper_coupling.shape, BF16),
            pltpu.VMEM(near_blocks.shape, BF16),
            pltpu.VMEM((RHS, leaves + 2 * W, cols, LEAF), BF16),
            pltpu.VMEM((leaves + 2 * W, cols, 2 * rank), BF16),
            pltpu.VMEM((leaves - 1, cols, 2 * rank), BF16),
            pltpu.VMEM((groups + 6, cols, 2 * rank), BF16),
            pltpu.VMEM((upper_rows, cols, 2 * rank), BF16),
            pltpu.VMEM((leaves, OPS * cols, rank), F32),
            pltpu.VMEM((2 * leaves, OPS * cols, rank), F32),
            pltpu.VMEM(near_shape, BF16),
            pltpu.VMEM(near_shape, BF16),
            pltpu.SemaphoreType.DMA((7,)),
            pltpu.SemaphoreType.DMA((17,)),
            pltpu.SemaphoreType.DMA((17,)),
            pltpu.SemaphoreType.DMA((groups - 1,)),
            pltpu.SemaphoreType.DMA((groups - 1,)),
            pltpu.SemaphoreType.DMA((CHUNKS, RHS)),
            pltpu.SemaphoreType.DMA((CHUNKS, RHS)),
        ],
        compiler_params=pltpu.CompilerParams(
            collective_id=0, has_side_effects=True, vmem_limit_bytes=56 * 1024 * 1024
        ),
        cost_estimate=pl.CostEstimate(
            flops=900_000_000, bytes_accessed=17_000_000, transcendentals=0
        ),
    )(
        points,
        near_offset,
        far_offset,
        leaf_basis,
        local_transfer,
        top_transfer,
        leaf_coupling,
        root_coupling,
        upper_coupling,
        near_blocks,
    )


def solution(mesh):
    placed = (
        P("rhs", "leaf"),
        P("leaf", None, None),
        P("leaf", None, None, None),
        P(),
        P(None, "leaf", None, None),
        P(None, "leaf", None, None),
        P(),
        P(None, "leaf", None, "rhs", None),
        P("leaf", None),
        P("leaf", None),
    )
    return jax.shard_map(
        per_device, mesh=mesh, in_specs=placed, out_specs=P(None, "rhs", "leaf"), check_vma=False
    )
```

time: 136 us -> 35.9 us (0.26)
  starting transfers between devices: 40 us -> 0 us
  local copies, waits for them, and re-layouts: 37.5 us -> 4.79 us
  Pallas kernels: 0 us -> 30.8 us
  matrix products: 22.5 us -> 0 us
  between operations: 13.9 us -> 0.01 us
  waiting for transfers between devices: 13.4 us -> 0 us
  other arithmetic: 7.29 us -> 0 us
    ppermute x13 -> x0, starting transfers between devices: 36.2 us -> none  [the longest x8 20.7 us: from_behind(): return lax.ppermute(block, axis, route)]
    pallas_call x0 -> x1, Pallas kernels: none -> 30.8 us  [per_device(): pl.pallas_call(functools.partial(kernel, groups), out_shape=jax.ShapeDtyp...]
    dot_general x16 -> x0, matrix products: 22.5 us -> none  [the longest x1 8.31 us: per_device(): jnp.einsum('ctkj,otkij->octi', all_columns, near_blocks, preferred_elemen...]
    all_to_all x1 -> x0, waiting for transfers between devices: 13.4 us -> none  [per_device(): lax.all_to_all(row_terms, 'rhs', split_axis=1, concat_axis=3, tiled=True)]
    all_to_all x3 -> x0, local copies, waits for them, and re-layouts: 9.45 us -> none  [per_device(): lax.all_to_all(row_terms, 'rhs', split_axis=1, concat_axis=3, tiled=True)]
    gather x4 -> x0, local copies, waits for them, and re-layouts: 7.26 us -> none  [the longest x1 3.94 us: per_device(): jnp.take(all_wide, near_index.reshape(-1), axis=1)]
    all_to_all x1 -> x0, other arithmetic: 6.37 us -> none  [per_device(): lax.all_to_all(row_terms, 'rhs', split_axis=1, concat_axis=3, tiled=True)]
    reshape x12 -> x0, local copies, waits for them, and re-layouts: 4.92 us -> none  [the longest x1 2.06 us: per_device(): return result.reshape(OPS, col_count, point_count)]
  transfers between devices with their start and end apart: 15 -> 0, of which waited for: 1 -> 0; matrix products, arithmetic and copies ran while one was open for 28% -> 0% of each run, Pallas kernels for 0% -> 0%
where the time goes in v1:
time: 35.9 us; the launch traced here: 35.6 us
  Pallas kernels  30.8 us (86%)
  local copies, waits for them, and re-layouts  4.79 us (13%)
    pallas_call x1, Pallas kernels, per_device(): pl.pallas_call(functools.partial(kernel, groups), out_shape=jax.ShapeDtyp...  30.8 us
    unnamed x3, local copies, waits for them, and re-layouts  4.79 us

profile of v1, /device:TPU:0, one launch (start us, length us, event | category | flops | bytes accessed | tf_op | source)
XLA Modules:
  0.0 35.6 jit_solution(14003746278653203515)
XLA Ops:
  0.0 1.4 %copy.11.near_offset = s32[32,3]{1,0:T(8,128)} copy(s32[32,3]{0,1:T(4,128)} %param.18) | data formatting | bytes 768 | tf_op args[8]
  1.4 1.4 %copy.12.far_offset = s32[32,5]{1,0:T(8,128)} copy(s32[32,5]{0,1:T(8,128)} %param.19) | data formatting | bytes 1280 | tf_op args[9]
  2.7 30.8 %shard_map.100 = bf16[3,16,8192]{2,1,0:T(8,128)(2,1)} custom-call(bf16[16,8192]{1,0:T(8,128)(2,1)} %points.1, s32[32,3]{1,0:T(8,128)} %copy.11.near_offset, s32[32,5]{1,0:T(8,128)} %copy.12.far_offset, bf16[32,64,256]{2,1,0:T(8,128)(2,1)} %basis_hbm.1, bf16[1,31,64,128]{3,2,1,0:T(8,128)(2,1)} %local_hbm.1, bf16[6,64,128]{2,1,0:T(8,128)(2,1)} %top_hbm.1, ...), custom_call_target="tpu_custom_call" | custom-call | flops 900000000 | bytes 17000000 | tf_op jit(solution)/shard_map/pallas_call | solution.py:430
  33.6 2.1 %copy.14 = bf16[3,16,8192]{2,1,0:T(8,128)(2,1)} copy(bf16[3,16,8192]{2,1,0:T(8,128)(2,1)} %shard_map.100) | data formatting | bytes 1572864

commit v2 on v1

--- a/solution.py
+++ b/solution.py
@@ -15,7 +15,7 @@
 TOPL = 3
 RHS = 4
 CHUNKS = 4
-UNROLL = 4
+UNROLL = 8
 MESH = pl.DeviceIdType.MESH
 F32 = jnp.float32
 BF16 = jnp.bfloat16
@@ -35,9 +35,9 @@
 
 def kernel(
     groups,
-    points,
-    near_offset,
-    far_offset,
+    points_hbm,
+    near_hbm,
+    far_hbm,
     basis_hbm,
     local_hbm,
     top_hbm,
@@ -45,6 +45,10 @@
     root_hbm,
     upper_hbm,
     blocks_hbm,
+    out_hbm,
+    points,
+    near_offset,
+    far_offset,
     out,
     basis,
     local,
@@ -60,6 +64,7 @@
     upper_coef,
     coupled,
     fields,
+    far_part,
     near_send,
     near_recv,
     in_sem,
@@ -69,6 +74,7 @@
     root_recv,
     near_ssem,
     near_rsem,
+    out_sem,
 ):
     cols = points.shape[0]
     leaves = basis.shape[0]
@@ -84,12 +90,23 @@
     has_right = me_l < groups - 1
     top_w = W + leaves
 
+    barrier = pltpu.get_barrier_semaphore()
+    for peer in peers[1:]:
+        pl.semaphore_signal(barrier, inc=1, device_id=(me_l, peer), device_id_type=MESH)
+    for step in range(1, groups):
+        pl.semaphore_signal(
+            barrier, inc=1, device_id=((me_l + step) % groups, me_r), device_id_type=MESH
+        )
+
     loads = [
         pltpu.make_async_copy(source, target, in_sem.at[i])
         for i, (source, target) in enumerate(
             [
+                (points_hbm, points),
                 (basis_hbm, basis),
                 (local_hbm, local),
+                (far_hbm, far_offset),
+                (near_hbm, near_offset),
                 (coupling_hbm, coupling),
                 (blocks_hbm, blocks),
                 (top_hbm, top),
@@ -101,16 +118,6 @@
     for load in loads:
         load.start()
 
-    barrier = pltpu.get_barrier_semaphore()
-    for peer in peers[1:]:
-        pl.semaphore_signal(barrier, inc=1, device_id=(me_l, peer), device_id_type=MESH)
-    for step in range(1, groups):
-        pl.semaphore_signal(
-            barrier, inc=1, device_id=((me_l + step) % groups, me_r), device_id_type=MESH
-        )
-
-    for t in range(leaves):
-        wide[0, W + t] = points[:, t * LEAF : (t + 1) * LEAF]
     low, high = pl.ds(0, W), pl.ds(top_w, W)
     head, tail = pl.ds(W, W), pl.ds(leaves, W)
     middle = pl.ds(2 * W, leaves - 2 * W)
@@ -129,6 +136,10 @@
     roots[0:3] = jnp.zeros((3, cols, 2 * rank), BF16)
     roots[3 + groups : 6 + groups] = jnp.zeros((3, cols, 2 * rank), BF16)
     upper_coef[...] = jnp.zeros(upper_coef.shape, BF16)
+
+    loads[0].wait()
+    for t in range(leaves):
+        wide[0, W + t] = points[:, t * LEAF : (t + 1) * LEAF]
 
     right = (me_l + 1) % groups
     left = (me_l + groups - 1) % groups
@@ -207,7 +218,7 @@
     def joined(a, b):
         return jnp.where(first_half, a.astype(F32), b.astype(F32)).astype(BF16)
 
-    loads[0].wait()
+    loads[1].wait()
 
     @pl.loop(0, leaves // UNROLL)
     def _(step):
@@ -225,7 +236,7 @@
     start(6)
     start(9)
 
-    loads[1].wait()
+    loads[2].wait()
     depth = leaves.bit_length() - 1
     offset = 0
     base = 0
@@ -258,32 +269,39 @@
     start(11)
     arrived(5)
     start(12)
+    arrived(2)
+    start(10)
     arrived(15)
     arrived(16)
 
-    loads[2].wait()
-
-    @pl.loop(0, leaves // UNROLL)
-    def _(step):
-        for u in range(UNROLL):
-            t = step * UNROLL + u
-            picked = [coef[W + t + far_offset[t, k]] for k in range(FAR)]
-            pieces = [joined(picked[k], picked[k + 1]) for k in range(0, FAR - 1, 2)]
-            pieces.append(picked[FAR - 1][:, :rank])
-            sources = jnp.concatenate(pieces, axis=-1)
-            for o in range(OPS):
-                coupled[t, o * cols : (o + 1) * cols] = dot_nt(sources, coupling[o, t])
-
+    for i in (3, 4, 5):
+        loads[i].wait()
+
+    def couple_leaves(begin, end):
+        @pl.loop(begin, end)
+        def _(step):
+            for u in range(UNROLL):
+                t = step * UNROLL + u
+                picked = [coef[W + t + far_offset[k, t]] for k in range(FAR)]
+                pieces = [joined(picked[k], picked[k + 1]) for k in range(0, FAR - 1, 2)]
+                pieces.append(picked[FAR - 1][:, :rank])
+                sources = jnp.concatenate(pieces, axis=-1)
+                matrix = coupling[:, t].reshape(OPS * rank, FAR * rank)
+                product = dot_nt(sources, matrix)
+                for o in range(OPS):
+                    coupled[t, o * cols : (o + 1) * cols] = product[:, o * rank : (o + 1) * rank]
+
+    steps = leaves // UNROLL
+    couple_leaves(0, steps // 2)
     arrived(6)
     start(13)
     arrived(7)
     start(14)
-    arrived(2)
-    start(10)
-    for number in (3, 8, 9, 11, 12, 13, 14, 10):
+    couple_leaves(steps // 2, steps)
+    for number in (3, 8, 9, 11, 12, 10, 13, 14):
         arrived(number)
 
-    loads[3].wait()
+    loads[6].wait()
     chunk_pairs = pairs // CHUNKS
 
     def near_copy(chunk, j):
@@ -300,15 +318,14 @@
     def near_leaf(t):
         total = None
         for k in range(NEAR):
-            left_side = wide[:, W + t + near_offset[t, k]].reshape(RHS * cols, LEAF)
+            left_side = wide[:, W + t + near_offset[k, t]].reshape(RHS * cols, LEAF)
             term = dot_nt(left_side, blocks[:, t, k].reshape(OPS * rank, LEAF))
             total = term if total is None else total + term
         return total
 
-    for chunk in range(CHUNKS):
-
-        @pl.loop(0, chunk_pairs)
-        def _(step):
+    @pl.loop(0, CHUNKS)
+    def _(chunk):
+        for step in range(chunk_pairs):
             pair = chunk * chunk_pairs + step
             first = near_leaf(2 * pair)
             second = near_leaf(2 * pair + 1)
@@ -330,7 +347,7 @@
 
     for step in range(1, groups):
         root_copy(step).wait_recv()
-    for i in (4, 5, 6):
+    for i in (7, 8, 9):
         loads[i].wait()
 
     def top_row(height):
@@ -378,28 +395,39 @@
             fields[2 * (count + p)] = pushed[:, :rank]
             fields[2 * (count + p) + 1] = pushed[:, rank:]
 
-    for j in range(1, RHS):
-        near_copy(0, j).wait_recv()
+    for t in range(leaves):
+        leaf_field = (fields[leaves + t] + coupled[t]).astype(BF16)
+        far_part[t] = dot_nn(leaf_field, basis[t])
+
     slots = (me_r, side, across, diagonal)
-    for chunk in range(CHUNKS):
-        if chunk:
-            for j in range(1, RHS):
-                near_copy(chunk, j).wait_recv()
-
+    chunk_points = 2 * chunk_pairs * LEAF
+
+    def out_copy(chunk):
+        where = pl.ds(pl.multiple_of(chunk * chunk_points, chunk_points), chunk_points)
+        return pltpu.make_async_copy(
+            out.at[chunk], out_hbm.at[:, :, where], out_sem.at[chunk]
+        )
+
+    @pl.loop(0, CHUNKS)
+    def _(chunk):
+        for j in range(1, RHS):
+            near_copy(chunk, j).wait_recv()
         for step in range(chunk_pairs):
             pair = chunk * chunk_pairs + step
             near = [near_recv[slots[r], pair].astype(F32) for r in range(RHS)]
             for e in range(2):
-                t = 2 * pair + e
-                leaf_field = (fields[leaves + t] + coupled[t]).astype(BF16)
-                far = dot_nn(leaf_field, basis[t])
+                place = 2 * step + e
+                far = far_part[2 * pair + e]
                 for o in range(OPS):
                     at = (2 * e + o if o < 2 else 4 + e) * rank
                     row = jnp.concatenate([piece[:, at : at + rank] for piece in near], axis=-1)
-                    out[o, :, t * LEAF : (t + 1) * LEAF] = (
+                    out[chunk, o, :, place * LEAF : (place + 1) * LEAF] = (
                         far[o * cols : (o + 1) * cols] + row
                     ).astype(BF16)
-
+        out_copy(chunk).start()
+
+    for chunk in range(CHUNKS):
+        out_copy(chunk).wait()
     for number in copies:
         run(number, "wait_send")
     for step in range(1, groups):
@@ -430,14 +458,13 @@
     return pl.pallas_call(
         functools.partial(kernel, groups),
         out_shape=jax.ShapeDtypeStruct((OPS, cols, count), BF16),
-        in_specs=[
-            pl.BlockSpec(memory_space=pltpu.VMEM),
-            pl.BlockSpec(memory_space=pltpu.SMEM),
-            pl.BlockSpec(memory_space=pltpu.SMEM),
-        ]
-        + [anywhere] * 7,
-        out_specs=pl.BlockSpec(memory_space=pltpu.VMEM),
+        in_specs=[anywhere] * 10,
+        out_specs=anywhere,
         scratch_shapes=[
+            pltpu.VMEM(points.shape, BF16),
+            pltpu.SMEM((NEAR, leaves), jnp.int32),
+            pltpu.SMEM((FAR, leaves), jnp.int32),
+            pltpu.VMEM((CHUNKS, OPS, cols, count // CHUNKS), BF16),
             pltpu.VMEM(leaf_basis.shape, BF16),
             pltpu.VMEM(local_transfer.shape, BF16),
             pltpu.VMEM(top_transfer.shape, BF16),
@@ -452,15 +479,17 @@
             pltpu.VMEM((upper_rows, cols, 2 * rank), BF16),
             pltpu.VMEM((leaves, OPS * cols, rank), F32),
             pltpu.VMEM((2 * leaves, OPS * cols, rank), F32),
+            pltpu.VMEM((leaves, OPS * cols, LEAF), F32),
             pltpu.VMEM(near_shape, BF16),
             pltpu.VMEM(near_shape, BF16),
-            pltpu.SemaphoreType.DMA((7,)),
+            pltpu.SemaphoreType.DMA((10,)),
             pltpu.SemaphoreType.DMA((17,)),
             pltpu.SemaphoreType.DMA((17,)),
             pltpu.SemaphoreType.DMA((groups - 1,)),
             pltpu.SemaphoreType.DMA((groups - 1,)),
             pltpu.SemaphoreType.DMA((CHUNKS, RHS)),
             pltpu.SemaphoreType.DMA((CHUNKS, RHS)),
+            pltpu.SemaphoreType.DMA((CHUNKS,)),
         ],
         compiler_params=pltpu.CompilerParams(
             collective_id=0, has_side_effects=True, vmem_limit_bytes=56 * 1024 * 1024
@@ -470,8 +499,8 @@
         ),
     )(
         points,
-        near_offset,
-        far_offset,
+        near_offset.T,
+        far_offset.T,
         leaf_basis,
         local_transfer,
         top_transfer,

time: 35.9 us -> 30.1 us (0.84)
  Pallas kernels: 30.8 us -> 27.9 us
  local copies, waits for them, and re-layouts: 4.79 us -> 2.06 us
    pallas_call x1, Pallas kernels: 30.8 us -> 27.9 us  [per_device(): pl.pallas_call(functools.partial(kernel, groups), out_shape=jax.ShapeDtyp...]
    unnamed x3 -> x1, local copies, waits for them, and re-layouts: 4.79 us -> 2.06 us
where the time goes in v2:
time: 30.1 us; the launch traced here: 30 us
  Pallas kernels  27.9 us (93%)
  local copies, waits for them, and re-layouts  2.06 us (7%)
    pallas_call x1, Pallas kernels, per_device(): pl.pallas_call(functools.partial(kernel, groups), out_shape=jax.ShapeDtyp...  27.9 us
    unnamed x1, local copies, waits for them, and re-layouts  2.06 us

profile of v2, /device:TPU:0, one launch (start us, length us, event | category | flops | bytes accessed | tf_op | source)
XLA Modules:
  0.0 30.0 jit_solution(13609468177482924121)
XLA Ops:
  0.0 27.9 %shard_map.100 = bf16[3,16,8192]{2,1,0:T(8,128)(2,1)} custom-call(bf16[16,8192]{1,0:T(8,128)(2,1)} %points_hbm.1, s32[3,32]{1,0:T(4,128)} %bitcast.3, s32[5,32]{1,0:T(8,128)} %bitcast.2, bf16[32,64,256]{2,1,0:T(8,128)(2,1)} %basis_hbm.1, bf16[1,31,64,128]{3,2,1,0:T(8,128)(2,1)} %local_hbm.1, bf16[6,64,128]{2,1,0:T(8,128)(2,1)} %top_hbm.1, ...), custom_call_target="tpu_custom_call" | custom-call | flops 900000000 | bytes 17000000 | tf_op jit(solution)/shard_map/pallas_call | solution.py:458
  27.9 2.1 %copy.12 = bf16[3,16,8192]{2,1,0:T(8,128)(2,1)} copy(bf16[3,16,8192]{2,1,0:T(8,128)(2,1)} %shard_map.100) | data formatting | bytes 1572864

commit v3 on v2

--- a/solution.py
+++ b/solution.py
@@ -14,7 +14,8 @@
 FAR = 5
 TOPL = 3
 RHS = 4
-CHUNKS = 4
+CHUNKS = 8
+PARTS = 2
 UNROLL = 8
 MESH = pl.DeviceIdType.MESH
 F32 = jnp.float32
@@ -437,6 +438,23 @@
             near_copy(chunk, j).wait_send()
 
 
+def handed_on(source, target, sems):
+    width = source.shape[2] // PARTS
+    copies = []
+    for o in range(OPS):
+        for part in range(PARTS):
+            piece = (o, slice(None), pl.ds(part * width, width))
+            copies.append(
+                pltpu.make_async_copy(
+                    source.at[piece], target.at[piece], sems.at[o * PARTS + part]
+                )
+            )
+    for copy in copies:
+        copy.start()
+    for copy in copies:
+        copy.wait()
+
+
 def per_device(
     points,
     leaf_basis,
@@ -455,7 +473,7 @@
     upper_rows = sum(groups // 2**h + 6 for h in range(1, TOPL))
     anywhere = pl.BlockSpec(memory_space=pl.ANY)
     near_shape = (RHS, leaves // 2, cols, 2 * OPS * rank)
-    return pl.pallas_call(
+    result = pl.pallas_call(
         functools.partial(kernel, groups),
         out_shape=jax.ShapeDtypeStruct((OPS, cols, count), BF16),
         in_specs=[anywhere] * 10,
@@ -509,6 +527,13 @@
         upper_coupling,
         near_blocks,
     )
+    return pl.pallas_call(
+        handed_on,
+        out_shape=jax.ShapeDtypeStruct(result.shape, BF16),
+        in_specs=[anywhere],
+        out_specs=anywhere,
+        scratch_shapes=[pltpu.SemaphoreType.DMA((OPS * PARTS,))],
+    )(result)
 
 
 def solution(mesh):

time: 30.1 us -> 53.3 us (1.77)
  Pallas kernels: 27.9 us -> 53.1 us
  local copies, waits for them, and re-layouts: 2.06 us -> 0 us
    pallas_call x0 -> x1, Pallas kernels: none -> 25 us  [per_device(): pl.pallas_call(handed_on, out_shape=jax.ShapeDtypeStruct(result.shape, BF...]
    unnamed x1 -> x0, local copies, waits for them, and re-layouts: 2.06 us -> none
where the time goes in v3:
time: 53.3 us; the launch traced here: 53.1 us
  Pallas kernels  53.1 us (100%)
    pallas_call x1, Pallas kernels, per_device(): pl.pallas_call(functools.partial(kernel, groups), out_shape=jax.ShapeDtyp...  28.1 us
    pallas_call x1, Pallas kernels, per_device(): pl.pallas_call(handed_on, out_shape=jax.ShapeDtypeStruct(result.shape, BF...  25 us

profile of v3, /device:TPU:0, one launch (start us, length us, event | category | flops | bytes accessed | tf_op | source)
XLA Modules:
  0.0 53.1 jit_solution(17993295891451053185)
XLA Ops:
  0.0 28.1 %shard_map.100.source = bf16[3,16,8192]{2,1,0:T(8,128)(2,1)} custom-call(bf16[16,8192]{1,0:T(8,128)(2,1)} %points_hbm.1, s32[3,32]{1,0:T(4,128)} %bitcast.3, s32[5,32]{1,0:T(8,128)} %bitcast.2, bf16[32,64,256]{2,1,0:T(8,128)(2,1)} %basis_hbm.1, bf16[1,31,64,128]{3,2,1,0:T(8,128)(2,1)} %local_hbm.1, bf16[6,64,128]{2,1,0:T(8,128)(2,1)} %top_hbm.1, ...), custom_call_target="tpu_custom_call" | custom-call | flops 900000000 | bytes 17000000 | tf_op jit(solution)/shard_map/pallas_call | solution.py:476
  28.1 25.0 %shard_map.101 = bf16[3,16,8192]{2,1,0:T(8,128)(2,1)} custom-call(bf16[3,16,8192]{2,1,0:T(8,128)(2,1)} %shard_map.100.source), custom_call_target="tpu_custom_call" | custom-call | tf_op jit(solution)/shard_map/pallas_call | solution.py:530

commit v4 on v2

--- a/solution.py
+++ b/solution.py
@@ -14,7 +14,7 @@
 FAR = 5
 TOPL = 3
 RHS = 4
-CHUNKS = 4
+CHUNKS = 8
 UNROLL = 8
 MESH = pl.DeviceIdType.MESH
 F32 = jnp.float32
@@ -93,10 +93,22 @@
     barrier = pltpu.get_barrier_semaphore()
     for peer in peers[1:]:
         pl.semaphore_signal(barrier, inc=1, device_id=(me_l, peer), device_id_type=MESH)
-    for step in range(1, groups):
-        pl.semaphore_signal(
-            barrier, inc=1, device_id=((me_l + step) % groups, me_r), device_id_type=MESH
-        )
+    near_by = (
+        (me_l - 2, me_l > 1),
+        (me_l - 1, me_l > 0),
+        (me_l + 1, me_l < groups - 1),
+        (me_l + 2, me_l < groups - 2),
+    )
+    greeted = len(peers) - 1
+    for neighbour, exists in near_by:
+        greeted += exists.astype(jnp.int32)
+
+        @pl.when(exists)
+        def _(neighbour=neighbour):
+            pl.semaphore_signal(
+                barrier, inc=1, device_id=(neighbour, me_r), device_id_type=MESH
+            )
+
 
     loads = [
         pltpu.make_async_copy(source, target, in_sem.at[i])
@@ -209,7 +221,7 @@
     def arrived(number):
         run(number, "wait_recv")
 
-    pl.semaphore_wait(barrier, len(peers) - 1 + groups - 1)
+    pl.semaphore_wait(barrier, greeted)
     for number in (0, 1, 4, 5, 2, 3):
         start(number)
 
@@ -252,18 +264,55 @@
         offset += count
     roots[3 + me_l] = level_coef[leaves - 2]
 
-    def root_copy(step):
+    pair_count = groups // 2
+    my_pair = me_l // 2
+    partner = me_l + 1 - 2 * (me_l % 2)
+
+    def root_swap():
         return pltpu.make_async_remote_copy(
             src_ref=roots.at[3 + me_l],
             dst_ref=roots.at[3 + me_l],
-            send_sem=root_send.at[step - 1],
-            recv_sem=root_recv.at[step - 1],
-            device_id=((me_l + step) % groups, me_r),
+            send_sem=root_send.at[0, 0],
+            recv_sem=root_recv.at[0, 0],
+            device_id=(partner, me_r),
             device_id_type=MESH,
         )
 
-    for step in range(1, groups):
-        root_copy(step).start()
+    def relay(distance, way, action):
+        sign = 1 - 2 * way
+        receiving = action == "wait_recv"
+        origin = my_pair - sign * (distance if receiving else distance - 1)
+        target = my_pair + sign
+        condition = jnp.logical_and(origin >= 0, origin < pair_count)
+        if not receiving:
+            condition = jnp.logical_and(
+                condition, jnp.logical_and(target >= 0, target < pair_count)
+            )
+
+        @pl.when(condition)
+        def _():
+            rows = pl.ds(3 + 2 * origin, 2)
+            copy = pltpu.make_async_remote_copy(
+                src_ref=roots.at[rows],
+                dst_ref=roots.at[rows],
+                send_sem=root_send.at[distance, way],
+                recv_sem=root_recv.at[distance, way],
+                device_id=(me_l + 2 * sign, me_r),
+                device_id_type=MESH,
+            )
+            getattr(copy, action)()
+
+    def relay_step(distance):
+        if distance == 1:
+            root_swap().wait_recv()
+        elif distance <= pair_count:
+            for way in range(2):
+                relay(distance - 1, way, "wait_recv")
+        if distance < pair_count:
+            for way in range(2):
+                relay(distance, way, "start")
+
+    root_swap().start()
 
     arrived(4)
     start(11)
@@ -293,11 +342,13 @@
 
     steps = leaves // UNROLL
     couple_leaves(0, steps // 2)
+    relay_step(1)
     arrived(6)
     start(13)
     arrived(7)
     start(14)
     couple_leaves(steps // 2, steps)
+    relay_step(2)
     for number in (3, 8, 9, 11, 12, 10, 13, 14):
         arrived(number)
 
@@ -323,8 +374,7 @@
             total = term if total is None else total + term
         return total
 
-    @pl.loop(0, CHUNKS)
-    def _(chunk):
+    def near_chunk(chunk):
         for step in range(chunk_pairs):
             pair = chunk * chunk_pairs + step
             first = near_leaf(2 * pair)
@@ -345,11 +395,6 @@
         for j in (2, 3, 1):
             near_copy(chunk, j).start()
 
-    for step in range(1, groups):
-        root_copy(step).wait_recv()
-    for i in (7, 8, 9):
-        loads[i].wait()
-
     def top_row(height):
         return groups - groups // 2 ** (height - 1)
 
@@ -361,7 +406,11 @@
             return roots[3 + index]
         return upper_coef[top_base(height) + 3 + index]
 
-    for height in range(1, TOPL):
+    def top_up():
+        for height in range(1, TOPL):
+            raise_level(height)
+
+    def raise_level(height):
         for q in range(groups // 2**height):
             pair = joined(top_coef(height - 1, 2 * q), top_coef(height - 1, 2 * q + 1))
             upper_coef[top_base(height) + 3 + q] = twice(dot_nt(pair, top[top_row(height) + q]))
@@ -379,21 +428,44 @@
             terms.append(dot_nt(sources, matrix))
         return jnp.concatenate(terms, axis=0)
 
-    running = top_field(TOPL - 1)
-    for height in range(TOPL - 1, 0, -1):
-        pushed = dot_nn(running.astype(BF16), top[top_row(height) + me_l // 2**height])
-        child = (me_l // 2 ** (height - 1)) % 2
-        half = jnp.where(child == 0, pushed[:, :rank], pushed[:, rank:])
-        running = top_field(height - 1) + half
-
-    fields[1] = running
-    for height in reversed(range(depth)):
+    def top_down():
+        running = top_field(TOPL - 1)
+        for height in range(TOPL - 1, 0, -1):
+            pushed = dot_nn(running.astype(BF16), top[top_row(height) + me_l // 2**height])
+            child = (me_l // 2 ** (height - 1)) % 2
+            half = jnp.where(child == 0, pushed[:, :rank], pushed[:, rank:])
+            running = top_field(height - 1) + half
+        fields[1] = running
+
+    def lower_level(height):
         count = leaves >> height + 1
         offset = leaves - 2 * count
         for p in range(count):
             pushed = dot_nn(fields[count + p].astype(BF16), local[0, offset + p])
             fields[2 * (count + p)] = pushed[:, :rank]
             fields[2 * (count + p) + 1] = pushed[:, rank:]
+
+    def lower_levels(high, low):
+        for height in range(high, low - 1, -1):
+            lower_level(height)
+
+    loaded = CHUNKS // 2
+    pl.loop(0, loaded // 2)(near_chunk)
+    relay_step(3)
+    pl.loop(loaded // 2, loaded)(near_chunk)
+    for distance in range(4, max(pair_count, 3) + 1):
+        relay_step(distance)
+    for i in (7, 8, 9):
+        loads[i].wait()
+    stages = (
+        top_up,
+        top_down,
+        functools.partial(lower_levels, depth - 1, 1),
+        functools.partial(lower_levels, 0, 0),
+    )
+    for chunk, stage in zip(range(loaded, CHUNKS), stages):
+        stage()
+        near_chunk(chunk)
 
     for t in range(leaves):
         leaf_field = (fields[leaves + t] + coupled[t]).astype(BF16)
@@ -430,11 +502,28 @@
         out_copy(chunk).wait()
     for number in copies:
         run(number, "wait_send")
-    for step in range(1, groups):
-        root_copy(step).wait_send()
+    root_swap().wait_send()
+    for distance in range(1, pair_count):
+        for way in range(2):
+            relay(distance, way, "wait_send")
     for chunk in range(CHUNKS):
         for j in range(1, RHS):
             near_copy(chunk, j).wait_send()
+
+
+def handed_on(source, target, held, sems):
+    ins = []
+    outs = []
+    for o in range(OPS):
+        ins.append(pltpu.make_async_copy(source.at[o], held.at[o], sems.at[0, o]))
+        outs.append(pltpu.make_async_copy(held.at[o], target.at[o], sems.at[1, o]))
+    for copy in ins:
+        copy.start()
+    for into, onward in zip(ins, outs):
+        into.wait()
+        onward.start()
+    for copy in outs:
+        copy.wait()
 
 
 def per_device(
@@ -455,7 +544,7 @@
     upper_rows = sum(groups // 2**h + 6 for h in range(1, TOPL))
     anywhere = pl.BlockSpec(memory_space=pl.ANY)
     near_shape = (RHS, leaves // 2, cols, 2 * OPS * rank)
-    return pl.pallas_call(
+    result = pl.pallas_call(
         functools.partial(kernel, groups),
         out_shape=jax.ShapeDtypeStruct((OPS, cols, count), BF16),
         in_specs=[anywhere] * 10,
@@ -485,8 +574,8 @@
             pltpu.SemaphoreType.DMA((10,)),
             pltpu.SemaphoreType.DMA((17,)),
             pltpu.SemaphoreType.DMA((17,)),
-            pltpu.SemaphoreType.DMA((groups - 1,)),
-            pltpu.SemaphoreType.DMA((groups - 1,)),
+            pltpu.SemaphoreType.DMA((groups // 2, 2)),
+            pltpu.SemaphoreType.DMA((groups // 2, 2)),
             pltpu.SemaphoreType.DMA((CHUNKS, RHS)),
             pltpu.SemaphoreType.DMA((CHUNKS, RHS)),
             pltpu.SemaphoreType.DMA((CHUNKS,)),
@@ -509,6 +598,16 @@
         upper_coupling,
         near_blocks,
     )
+    return pl.pallas_call(
+        handed_on,
+        out_shape=jax.ShapeDtypeStruct(result.shape, BF16),
+        in_specs=[anywhere],
+        out_specs=anywhere,
+        scratch_shapes=[
+            pltpu.VMEM(result.shape, BF16),
+            pltpu.SemaphoreType.DMA((2, OPS)),
+        ],
+    )(result)
 
 
 def solution(mesh):

time: 30.1 us -> 32.3 us (1.073)
  Pallas kernels: 27.9 us -> 32.2 us
  local copies, waits for them, and re-layouts: 2.06 us -> 0 us
    pallas_call x1, Pallas kernels: 27.9 us -> 30.3 us  [per_device(): pl.pallas_call(functools.partial(kernel, groups), out_shape=jax.ShapeDtyp...]
    unnamed x1 -> x0, local copies, waits for them, and re-layouts: 2.06 us -> none
    pallas_call x0 -> x1, Pallas kernels: none -> 1.88 us  [per_device(): pl.pallas_call(handed_on, out_shape=jax.ShapeDtypeStruct(result.shape, BF...]
where the time goes in v4:
time: 32.3 us; the launch traced here: 32.2 us
  Pallas kernels  32.2 us (100%)
    pallas_call x1, Pallas kernels, per_device(): pl.pallas_call(functools.partial(kernel, groups), out_shape=jax.ShapeDtyp...  30.3 us
    pallas_call x1, Pallas kernels, per_device(): pl.pallas_call(handed_on, out_shape=jax.ShapeDtypeStruct(result.shape, BF...  1.88 us

profile of v4, /device:TPU:0, one launch (start us, length us, event | category | flops | bytes accessed | tf_op | source)
XLA Modules:
  0.0 32.2 jit_solution(3182758005790776663)
XLA Ops:
  0.0 30.3 %shard_map.100.source = bf16[3,16,8192]{2,1,0:T(8,128)(2,1)} custom-call(bf16[16,8192]{1,0:T(8,128)(2,1)} %points_hbm.1, s32[3,32]{1,0:T(4,128)} %bitcast.3, s32[5,32]{1,0:T(8,128)} %bitcast.2, bf16[32,64,256]{2,1,0:T(8,128)(2,1)} %basis_hbm.1, bf16[1,31,64,128]{3,2,1,0:T(8,128)(2,1)} %local_hbm.1, bf16[6,64,128]{2,1,0:T(8,128)(2,1)} %top_hbm.1, ...), custom_call_target="tpu_custom_call" | custom-call | flops 900000000 | bytes 17000000 | tf_op jit(solution)/shard_map/pallas_call | solution.py:547
  30.3 1.9 %shard_map.101 = bf16[3,16,8192]{2,1,0:T(8,128)(2,1)} custom-call(bf16[3,16,8192]{2,1,0:T(8,128)(2,1)} %shard_map.100.source), custom_call_target="tpu_custom_call" | custom-call | tf_op jit(solution)/shard_map/pallas_call | solution.py:601

commit v5 on v2

--- a/solution.py
+++ b/solution.py
@@ -316,12 +316,11 @@
         )
 
     def near_leaf(t):
-        total = None
-        for k in range(NEAR):
-            left_side = wide[:, W + t + near_offset[k, t]].reshape(RHS * cols, LEAF)
-            term = dot_nt(left_side, blocks[:, t, k].reshape(OPS * rank, LEAF))
-            total = term if total is None else total + term
-        return total
+        sources = [
+            wide[:, W + t + near_offset[k, t]].reshape(RHS * cols, LEAF) for k in range(NEAR)
+        ]
+        matrices = [blocks[:, t, k].reshape(OPS * rank, LEAF) for k in range(NEAR)]
+        return dot_nt(jnp.concatenate(sources, axis=-1), jnp.concatenate(matrices, axis=-1))
 
     @pl.loop(0, CHUNKS)
     def _(chunk):

time: 30.1 us -> 30.1 us (level)
  no operation moved by 1% of the time
where the time goes in v5:
time: 30.1 us; the launch traced here: 30 us
  Pallas kernels  27.9 us (93%)
  local copies, waits for them, and re-layouts  2.06 us (7%)
    pallas_call x1, Pallas kernels, per_device(): pl.pallas_call(functools.partial(kernel, groups), out_shape=jax.ShapeDtyp...  27.9 us
    unnamed x1, local copies, waits for them, and re-layouts  2.06 us

profile of v5, /device:TPU:0, one launch (start us, length us, event | category | flops | bytes accessed | tf_op | source)
XLA Modules:
  0.0 30.0 jit_solution(2805044412835031625)
XLA Ops:
  0.0 27.9 %shard_map.100 = bf16[3,16,8192]{2,1,0:T(8,128)(2,1)} custom-call(bf16[16,8192]{1,0:T(8,128)(2,1)} %points_hbm.1, s32[3,32]{1,0:T(4,128)} %bitcast.3, s32[5,32]{1,0:T(8,128)} %bitcast.2, bf16[32,64,256]{2,1,0:T(8,128)(2,1)} %basis_hbm.1, bf16[1,31,64,128]{3,2,1,0:T(8,128)(2,1)} %local_hbm.1, bf16[6,64,128]{2,1,0:T(8,128)(2,1)} %top_hbm.1, ...), custom_call_target="tpu_custom_call" | custom-call | flops 900000000 | bytes 17000000 | tf_op jit(solution)/shard_map/pallas_call | solution.py:457
  27.9 2.1 %copy.12 = bf16[3,16,8192]{2,1,0:T(8,128)(2,1)} copy(bf16[3,16,8192]{2,1,0:T(8,128)(2,1)} %shard_map.100) | data formatting | bytes 1572864
